TPU v7x, 32 devices: a whole 2x2x4 slice. The times are simulated.
32 devices in a mesh: wide: 8 (over z, core), narrow: 4 (over y, x).
Axes of the slice: x: 2, y: 2, z: 4, core: 2. Of those that a mesh axis runs over, the one named last changes fastest.
Arguments:
- video: bfloat16 [32, 11, 64, 512], P(('wide', 'narrow')), may hold values from -6 to 6
- frames: int32 [32], P(('wide', 'narrow')), may hold values from 1 to 21, as said below
- cotangent: bfloat16 [32, 11, 64, 512], P(('wide', 'narrow')), may hold values from -6 to 6
- qkv_weight: float32 [2, 512, 1536], P(None, ('wide', 'narrow')), may hold values from -0.25 to 0.25
- out_weight: float32 [2, 512, 512], P(None, ('wide', 'narrow')), may hold values from -0.75 to 0.75
- in_weight: float32 [2, 512, 2048], P(None, ('wide', 'narrow')), may hold values from -0.25 to 0.25
- down_weight: float32 [2, 2048, 512], P(None, ('wide', 'narrow')), may hold values from -0.125 to 0.125
- attn_gain: float32 [2, 512], P(None, ('wide', 'narrow')), may hold values from 0.25 to 1.75
- mlp_gain: float32 [2, 512], P(None, ('wide', 'narrow')), may hold values from 0.25 to 1.75
Outputs:
- output: bfloat16 [32, 11, 64, 512], P(('wide', 'narrow'))
- grad_video: bfloat16 [32, 11, 64, 512], P(('wide', 'narrow'))
- grad_qkv: float32 [2, 512, 1536], P(None, ('wide', 'narrow'))
- grad_out: float32 [2, 512, 512], P(None, ('wide', 'narrow'))
- grad_in: float32 [2, 512, 2048], P(None, ('wide', 'narrow'))
- grad_down: float32 [2, 2048, 512], P(None, ('wide', 'narrow'))
- grad_attn_gain: float32 [2, 512], P(None, ('wide', 'narrow'))
- grad_mlp_gain: float32 [2, 512], P(None, ('wide', 'narrow'))
Inputs may be any that keep to these rules, and one draw needn't show every extreme that they name: Every draw has a clip of 21 frames and a clip of 1 frame.
All inputs are finite; a program needn't handle non-finite values.
Results may differ from a plain program's by a relative error of at most 0.02.
Values may be sent and summed in bfloat16 or wider, within the bound.
A program may use at most 192 MiB of HBM per device.

v0:
```python
import jax
import jax.numpy as jnp
from jax import lax
from jax.sharding import PartitionSpec as P

HEADS = 8


epsilon = 1e-05


def norm_rows(inputs, scaling):
    centre = jnp.mean(inputs, axis=-1, keepdims=True)
    centred = inputs - centre
    spread = jnp.mean(centred * centred, axis=-1, keepdims=True)
    return centred * lax.rsqrt(spread + epsilon) * scaling


def project(rows_in, matrix):
    return jnp.einsum("cspd,de->cspe", rows_in, matrix, preferred_element_type=jnp.float32)


def project_back(rows_in, matrix):
    return jnp.einsum("cspe,de->cspd", rows_in, matrix, preferred_element_type=jnp.float32)


def weight_grad(left, right):
    return jnp.einsum("cspd,cspe->de", left, right, preferred_element_type=jnp.float32)


def pair_scores(first, second, which_block):
    if which_block == 0:
        return jnp.einsum("csphe,csqhe->cshpq", first, second, preferred_element_type=jnp.float32)
    return jnp.einsum("csphe,ctphe->cphst", first, second, preferred_element_type=jnp.float32)


def pair_mix(weighting, second, which_block):
    if which_block == 0:
        return jnp.einsum(
            "cshpq,csqhe->csphe", weighting, second, preferred_element_type=jnp.float32
        )
    return jnp.einsum("cphst,ctphe->csphe", weighting, second, preferred_element_type=jnp.float32)


def pair_back(weighting, first, which_block):
    if which_block == 0:
        return jnp.einsum(
            "cshpq,csphe->csqhe", weighting, first, preferred_element_type=jnp.float32
        )
    return jnp.einsum("cphst,csphe->ctphe", weighting, first, preferred_element_type=jnp.float32)


def masked_scores(queries, key_rows, which_block, allowed):
    head_size = queries.shape[-1]
    scores = pair_scores(queries, key_rows, which_block) * head_size ** (-0.5)
    if which_block == 1:
        scores = jnp.where(allowed[:, None, None], scores, -1000000000.0)
    return scores


def block_forward(inputs, weights, which_block, allowed):
    qkv_matrix, out_matrix, in_matrix, down_matrix, attn_scaling, mlp_scaling = weights
    full_shape = inputs.shape
    head_size = full_shape[-1] // HEADS
    normed, norm_pull = jax.vjp(norm_rows, inputs, attn_scaling.astype(jnp.float32))
    normed_low = normed.astype(jnp.bfloat16)
    qkv_rows = project(normed_low, qkv_matrix).astype(jnp.bfloat16)
    split = qkv_rows.reshape(full_shape[:3] + (3, HEADS, head_size))
    queries = split[:, :, :, 0]
    key_rows = split[:, :, :, 1]
    value_rows = split[:, :, :, 2]
    scores = masked_scores(queries, key_rows, which_block, allowed)
    row_max = jnp.max(scores, axis=-1, keepdims=True)
    shifted = jnp.exp(scores - row_max)
    row_sum = jnp.sum(shifted, axis=-1, keepdims=True)
    log_total = row_max + jnp.log(row_sum)
    probs_low = (shifted / row_sum).astype(jnp.bfloat16)
    attended = pair_mix(probs_low, value_rows, which_block).reshape(full_shape).astype(jnp.bfloat16)
    middle = inputs + project(attended, out_matrix)
    normed_mlp, mlp_pull = jax.vjp(norm_rows, middle, mlp_scaling.astype(jnp.float32))
    normed_mlp_low = normed_mlp.astype(jnp.bfloat16)
    hidden = project(normed_mlp_low, in_matrix)
    active, gelu_pull = jax.vjp(jax.nn.gelu, hidden)
    active_low = active.astype(jnp.bfloat16)
    result = middle + project(active_low, down_matrix)
    stored = (
        norm_pull,
        normed_low,
        queries,
        key_rows,
        value_rows,
        log_total,
        attended,
        mlp_pull,
        normed_mlp_low,
        gelu_pull,
        active_low,
    )
    return (result, stored)


def block_backward(gradient, stored, weights, which_block, allowed):
    qkv_matrix, out_matrix, in_matrix, down_matrix, attn_scaling, mlp_scaling = weights
    (
        norm_pull,
        normed_low,
        queries,
        key_rows,
        value_rows,
        log_total,
        attended,
        mlp_pull,
        normed_mlp_low,
        gelu_pull,
        active_low,
    ) = stored
    full_shape = gradient.shape
    head_size = queries.shape[-1]
    result_low = gradient.astype(jnp.bfloat16)
    grad_down_w = weight_grad(active_low, result_low)
    grad_active = project_back(result_low, down_matrix)
    grad_hidden = gelu_pull(grad_active)[0].astype(jnp.bfloat16)
    grad_in_w = weight_grad(normed_mlp_low, grad_hidden)
    grad_normed_mlp = project_back(grad_hidden, in_matrix)
    middle_part, grad_mlp_scaling = mlp_pull(grad_normed_mlp)
    grad_middle = gradient + middle_part
    middle_low = grad_middle.astype(jnp.bfloat16)
    grad_out_w = weight_grad(attended, middle_low)
    grad_attended = project_back(middle_low, out_matrix).astype(jnp.bfloat16)
    grad_attended = grad_attended.reshape(queries.shape)
    scores = masked_scores(queries, key_rows, which_block, allowed)
    soft_probs = jnp.exp(scores - log_total)
    grad_probs = pair_scores(grad_attended, value_rows, which_block)
    row_delta = jnp.sum(grad_probs * soft_probs, axis=-1, keepdims=True)
    grad_scores = (soft_probs * (grad_probs - row_delta)).astype(jnp.bfloat16)
    score_scale = head_size ** (-0.5)
    grad_queries = pair_mix(grad_scores, key_rows, which_block) * score_scale
    grad_keys = pair_back(grad_scores, queries, which_block) * score_scale
    grad_values = pair_back(soft_probs.astype(jnp.bfloat16), grad_attended, which_block)
    grad_qkv_rows = jnp.stack([grad_queries, grad_keys, grad_values], axis=3).astype(jnp.bfloat16)
    grad_qkv_rows = grad_qkv_rows.reshape(full_shape[:3] + (3 * full_shape[-1],))
    grad_qkv_w = weight_grad(normed_low, grad_qkv_rows)
    grad_normed = project_back(grad_qkv_rows, qkv_matrix)
    input_part, grad_attn_scaling = norm_pull(grad_normed)
    grad_input = grad_middle + input_part
    return (
        grad_input,
        (grad_qkv_w, grad_out_w, grad_in_w, grad_down_w, grad_attn_scaling, grad_mlp_scaling),
    )


def block_shards(qkv_weight, out_weight, in_weight, down_weight, attn_gain, mlp_gain, block_index):
    return (
        qkv_weight[block_index].astype(jnp.bfloat16),
        out_weight[block_index].astype(jnp.bfloat16),
        in_weight[block_index].astype(jnp.bfloat16),
        down_weight[block_index].astype(jnp.bfloat16),
        attn_gain[block_index].astype(jnp.bfloat16),
        mlp_gain[block_index].astype(jnp.bfloat16),
    )


def pair_stack(first, second):
    return tuple((jnp.stack([first[number], second[number]]) for number in range(6)))


def shards(
    video, frames, cotangent, qkv_weight, out_weight, in_weight, down_weight, attn_gain, mlp_gain
):
    slot_counts = (frames + 1) // 2
    positions = jnp.arange(video.shape[1], dtype=jnp.int32)
    allowed = (positions[None, None, :] <= positions[None, :, None]) & (
        positions[None, None, :] < slot_counts[:, None, None]
    )
    valid_slot = (positions[None, :] < slot_counts[:, None]).astype(jnp.float32)[:, :, None, None]
    spatial_parts = block_shards(
        qkv_weight, out_weight, in_weight, down_weight, attn_gain, mlp_gain, 0
    )
    temporal_parts = block_shards(
        qkv_weight, out_weight, in_weight, down_weight, attn_gain, mlp_gain, 1
    )
    spatial_full = (
        lax.all_gather(spatial_parts[0], ("wide", "narrow"), axis=0, tiled=True),
        lax.all_gather(spatial_parts[1], ("wide", "narrow"), axis=0, tiled=True),
        lax.all_gather(spatial_parts[2], ("wide", "narrow"), axis=0, tiled=True),
        lax.all_gather(spatial_parts[3], ("wide", "narrow"), axis=0, tiled=True),
        lax.all_gather(spatial_parts[4], ("wide", "narrow"), axis=0, tiled=True),
        lax.all_gather(spatial_parts[5], ("wide", "narrow"), axis=0, tiled=True),
    )
    temporal_full = (
        lax.all_gather(temporal_parts[0], ("wide", "narrow"), axis=0, tiled=True),
        lax.all_gather(temporal_parts[1], ("wide", "narrow"), axis=0, tiled=True),
        lax.all_gather(temporal_parts[2], ("wide", "narrow"), axis=0, tiled=True),
        lax.all_gather(temporal_parts[3], ("wide", "narrow"), axis=0, tiled=True),
        lax.all_gather(temporal_parts[4], ("wide", "narrow"), axis=0, tiled=True),
        lax.all_gather(temporal_parts[5], ("wide", "narrow"), axis=0, tiled=True),
    )
    start_rows = video.astype(jnp.float32)
    spatial_out, spatial_stored = block_forward(start_rows, spatial_full, 0, allowed)
    temporal_out, temporal_stored = block_forward(spatial_out, temporal_full, 1, allowed)
    output = (temporal_out * valid_slot).astype(jnp.bfloat16)
    gradient = cotangent.astype(jnp.float32) * valid_slot
    temporal_back = (
        lax.all_gather(temporal_parts[0], ("wide", "narrow"), axis=0, tiled=True),
        lax.all_gather(temporal_parts[1], ("wide", "narrow"), axis=0, tiled=True),
        lax.all_gather(temporal_parts[2], ("wide", "narrow"), axis=0, tiled=True),
        lax.all_gather(temporal_parts[3], ("wide", "narrow"), axis=0, tiled=True),
        lax.all_gather(temporal_parts[4], ("wide", "narrow"), axis=0, tiled=True),
        lax.all_gather(temporal_parts[5], ("wide", "narrow"), axis=0, tiled=True),
    )
    grad_between, temporal_grads = block_backward(
        gradient, temporal_stored, temporal_back, 1, allowed
    )
    spatial_back = (
        lax.all_gather(spatial_parts[0], ("wide", "narrow"), axis=0, tiled=True),
        lax.all_gather(spatial_parts[1], ("wide", "narrow"), axis=0, tiled=True),
        lax.all_gather(spatial_parts[2], ("wide", "narrow"), axis=0, tiled=True),
        lax.all_gather(spatial_parts[3], ("wide", "narrow"), axis=0, tiled=True),
        lax.all_gather(spatial_parts[4], ("wide", "narrow"), axis=0, tiled=True),
        lax.all_gather(spatial_parts[5], ("wide", "narrow"), axis=0, tiled=True),
    )
    grad_start, spatial_grads = block_backward(
        grad_between, spatial_stored, spatial_back, 0, allowed
    )
    stacked = pair_stack(spatial_grads, temporal_grads)
    summed = (
        lax.psum_scatter(stacked[0], ("wide", "narrow"), scatter_dimension=1, tiled=True),
        lax.psum_scatter(stacked[1], ("wide", "narrow"), scatter_dimension=1, tiled=True),
        lax.psum_scatter(stacked[2], ("wide", "narrow"), scatter_dimension=1, tiled=True),
        lax.psum_scatter(stacked[3], ("wide", "narrow"), scatter_dimension=1, tiled=True),
        lax.psum_scatter(stacked[4], ("wide", "narrow"), scatter_dimension=1, tiled=True),
        lax.psum_scatter(stacked[5], ("wide", "narrow"), scatter_dimension=1, tiled=True),
    )
    return (
        output,
        grad_start.astype(jnp.bfloat16),
        summed[0],
        summed[1],
        summed[2],
        summed[3],
        summed[4],
        summed[5],
    )


def solution(mesh):
    in_specs = (
        P(("wide", "narrow"), None, None, None),
        P(("wide", "narrow")),
        P(("wide", "narrow"), None, None, None),
        P(None, ("wide", "narrow"), None),
        P(None, ("wide", "narrow"), None),
        P(None, ("wide", "narrow"), None),
        P(None, ("wide", "narrow"), None),
        P(None, ("wide", "narrow")),
        P(None, ("wide", "narrow")),
    )
    out_specs = (
        P(("wide", "narrow"), None, None, None),
        P(("wide", "narrow"), None, None, None),
        P(None, ("wide", "narrow"), None),
        P(None, ("wide", "narrow"), None),
        P(None, ("wide", "narrow"), None),
        P(None, ("wide", "narrow"), None),
        P(None, ("wide", "narrow")),
        P(None, ("wide", "narrow")),
    )
    return jax.shard_map(shards, mesh=mesh, in_specs=in_specs, out_specs=out_specs, check_vma=False)
```

profile of v0, /device:TPU:0, one launch (start us, length us, event | category | flops | bytes accessed | tf_op | source)
XLA Modules:
  0.0 1355.5 jit_solution(9568224420658574559)
XLA Ops:
  16.3 42.2 %all-reduce.4 = (bf16[512]{0:T(512)(128)(2,1)S(1)}, bf16[512]{0:T(512)(128)(2,1)S(1)}, bf16[512]{0:T(512)(128)(2,1)S(1)}, bf16[512]{0:T(512)(128)(2,1)S(1)}) all-reduce(bf16[512]{0:T(512)(128)(2,1)S(1)} %dynamic-update-slice, bf16[512]{0:T(512)(128)(2,1)S(1)} %dynamic-update-slice.1, ...), channel_id=2, replica_groups=mesh['wide'=8,'narrow'=4] {'wide','narrow'}, use_global_device_ids=true, to_apply=%add | all-reduce | flops 2048 | bytes 8192
  59.8 74.6 %all-gather.8 = bf16[1,512,512]{2,1,0:T(8,128)(2,1)} all-gather(bf16[1,16,512]{2,1,0:T(8,128)(2,1)S(1)} %get-tuple-element.38), channel_id=10, replica_groups=mesh['wide'=8,'narrow'=4] {'wide','narrow'}, dimensions={1}, use_global_device_ids=true | all-gather | bytes 540672 | tf_op jit(solution)/shard_map/all_gather | solution.py:192
  134.4 67.0 %all-gather.2 = bf16[1,512,512]{2,1,0:T(8,128)(2,1)S(1)} all-gather(bf16[1,16,512]{2,1,0:T(8,128)(2,1)S(1)} %get-tuple-element.39), channel_id=4, replica_groups=mesh['wide'=8,'narrow'=4] {'wide','narrow'}, dimensions={1}, use_global_device_ids=true | all-gather | bytes 540672 | tf_op jit(solution)/shard_map/all_gather | solution.py:184
  204.4 3.9 reshape.716
  208.3 4.3 fusion.129
  222.0 6.2 fusion.37
  228.2 5.9 fusion.135
  235.7 9.9 all-gather.25.cloned.1.call-done
  245.6 4.5 convolution_convert_fusion
  250.1 6.5 reshape.722
  256.7 3.7 fusion.128
  262.0 3.9 fusion.23
  265.9 3.9 copy.103
  271.8 5.3 copy.104
  281.6 3.1 convert_element_type.238
  289.2 15.0 %all-gather.27.cloned.1.call-done = bf16[1,512,2048]{2,1,0:T(8,128)(2,1)} async-done(((bf16[1,16,2048]{2,1,0:T(8,128)(2,1)}), bf16[1,512,2048]{2,1,0:T(8,128)(2,1)}) %all-gather.27.cloned.1.call-update) | async-done | bytes 2097168 | tf_op jit(solution)/shard_map/all_gather | solution.py:193
  304.2 6.2 fusion.30
  310.4 52.4 %all-gather.29.cloned.1.call-done = bf16[1,2048,512]{2,1,0:T(8,128)(2,1)} async-done(((bf16[1,64,512]{2,1,0:T(8,128)(2,1)}), bf16[1,2048,512]{2,1,0:T(8,128)(2,1)}) %all-gather.29.cloned.1.call-update) | async-done | bytes 2097168 | tf_op jit(solution)/shard_map/all_gather | solution.py:194
  362.8 7.8 fusion.13
  381.1 5.8 fusion.17
  386.9 4.4 copy.108
  394.7 5.2 copy.110
  399.9 5.0 fusion.44
  407.4 4.5 copy.112
  412.0 3.2 convert_bitcast_fusion
  417.2 3.2 copy.113
  420.4 6.5 convert_element_type.255
  427.0 4.0 fusion.70
  434.3 5.0 fusion.6
  449.3 3.5 fusion.52
  460.9 5.3 copy.125
  466.2 6.6 convert_element_type.262
  472.8 3.5 fusion.65
  480.9 3.3 convolution_bitcast_fusion.1
  485.8 3.1 pad_maximum_fusion.3
  490.3 4.0 convolution_bitcast_fusion.4
  496.4 3.9 pad_maximum_fusion
  500.3 4.9 convolution_bitcast_fusion.2
  505.2 4.4 convolution_bitcast_fusion.3
  509.6 4.2 pad_maximum_fusion.1
  515.0 3.4 add_convert_fusion
  518.4 5.6 multiply_convert_fusion.7
  524.0 66.7 %reduce-scatter.21.cloned.1.call-done = f32[16,2]{1,0:T(8,128)} async-done(((f32[512,2]{1,0:T(8,128)}), f32[16,2]{1,0:T(8,128)}) %reduce-scatter.21.cloned.1.call-update) | async-done | bytes 144
  592.0 130.5 %reduce-scatter.19.cloned.1.call-done = f32[16,2]{1,0:T(8,128)} async-done(((f32[512,2]{1,0:T(8,128)}), f32[16,2]{1,0:T(8,128)}) %reduce-scatter.19.cloned.1.call-update) | async-done | bytes 144
  723.8 134.4 %reduce-scatter.13.cloned.1.call-done = f32[2,16,512]{2,1,0:T(8,128)} async-done(((f32[2,512,512]{2,1,0:T(8,128)}), f32[2,16,512]{2,1,0:T(8,128)}) %reduce-scatter.13.cloned.1.call-update) | async-done | bytes 65552 | tf_op jit(solution)/shard_map/reduce_scatter | solution.py:228
  858.2 117.4 %reduce-scatter.11.cloned.1.call-done = f32[2,16,1536]{2,1,0:T(8,128)} async-done(((f32[2,512,1536]{2,1,0:T(8,128)}), f32[2,16,1536]{2,1,0:T(8,128)}) %reduce-scatter.11.cloned.1.call-update) | async-done | bytes 196624 | tf_op jit(solution)/shard_map/reduce_scatter | solution.py:227
  975.6 185.7 %reduce-scatter.15.cloned.1.call-done = f32[2,16,2048]{2,1,0:T(8,128)} async-done(((f32[2,512,2048]{2,1,0:T(8,128)}), f32[2,16,2048]{2,1,0:T(8,128)}) %reduce-scatter.15.cloned.1.call-update) | async-done | bytes 262160 | tf_op jit(solution)/shard_map/reduce_scatter | solution.py:229
  1161.3 187.2 %reduce-scatter.17.cloned.1.call-done = f32[2,64,512]{2,1,0:T(8,128)} async-done(((f32[2,2048,512]{2,1,0:T(8,128)}), f32[2,64,512]{2,1,0:T(8,128)}) %reduce-scatter.17.cloned.1.call-update) | async-done | bytes 262160 | tf_op jit(solution)/shard_map/reduce_scatter | solution.py:230
  (293 shorter events, 88.5 us)
Async XLA Ops:
  7.2 8.2 copy-start.81
  7.2 8.2 copy-start.82
  7.2 51.9 %copy-start.13 = (bf16[1,11,64,512]{3,2,1,0:T(8,128)(2,1)S(1)}, bf16[1,11,64,512]{3,2,1,0:T(8,128)(2,1)}, u32[]{:S(2)}) copy-start(bf16[1,11,64,512]{3,2,1,0:T(8,128)(2,1)} %param.9) | copy-start | bytes 2162692
  7.2 194.2 %all-gather.19.cloned.1.call-start = ((), (), s32[]{:S(2)}) async-start(), calls=%async_computation.10 | async-start | bytes 1622016 | tf_op jit(solution)/shard_map/all_gather | solution.py:183
  8.9 50.8 %copy-start.71 = (f32[2,16,512]{2,1,0:T(8,128)S(1)}, f32[2,16,512]{2,1,0:T(8,128)}, u32[]{:S(2)}) copy-start(f32[2,16,512]{2,1,0:T(8,128)} %param.13) | copy-start | bytes 196612
  8.9 213.1 %all-gather.21.cloned.1.call-start = ((), (), s32[]{:S(2)}) async-start(), calls=%async_computation.11 | async-start | bytes 2162688 | tf_op jit(solution)/shard_map/all_gather | solution.py:185
  10.6 217.6 %all-gather.23.cloned.1.call-start = ((), (), s32[]{:S(2)}) async-start(), calls=%async_computation.12 | async-start | bytes 2162688 | tf_op jit(solution)/shard_map/all_gather | solution.py:186
  12.3 233.2 %all-gather.25.cloned.1.call-start = ((), (), s32[]{:S(2)}) async-start(), calls=%async_computation.13 | async-start | bytes 1622016 | tf_op jit(solution)/shard_map/all_gather | solution.py:191
  12.9 291.3 %all-gather.27.cloned.1.call-start = ((), (), s32[]{:S(2)}) async-start(), calls=%async_computation.14 | async-start | bytes 2162688 | tf_op jit(solution)/shard_map/all_gather | solution.py:193
  13.5 349.3 %all-gather.29.cloned.1.call-start = ((), (), s32[]{:S(2)}) async-start(), calls=%async_computation.15 | async-start | bytes 2162688 | tf_op jit(solution)/shard_map/all_gather | solution.py:194
  14.1 576.5 %reduce-scatter.21.cloned.1.call-start = ((), (), s32[]{:S(2)}) async-start(), calls=%async_computation.17 | async-start | bytes 270336
  58.5 145.8 %copy-start.74 = (f32[512]{0:T(512)}, f32[512]{0:T(512)S(1)}, u32[]{:S(2)}) copy-start(f32[512]{0:T(512)S(1)} %convert_element_type.268) | copy-start | bytes 6148
  58.5 211.7 %copy-start.59 = (pred[11,11]{1,0:T(8,128)(4,1)}, pred[11,11]{1,0:T(8,128)(4,1)S(1)}, u32[]{:S(2)}) copy-start(pred[11,11]{1,0:T(8,128)(4,1)S(1)} %fusion.118) | copy-start | bytes 367
  58.5 187.1 %copy-start.72 = (f32[512]{0:T(512)}, f32[512]{0:T(512)S(1)}, u32[]{:S(2)}) copy-start(f32[512]{0:T(512)S(1)} %convert_element_type.270) | copy-start | bytes 6148
  59.3 145.0 %copy-start.49 = (f32[11,64]{1,0:T(8,128)}, f32[11,64]{1,0:T(8,128)S(1)}, u32[]{:S(2)}) copy-start(f32[11,64]{1,0:T(8,128)S(1)} %broadcast_multiply_fusion.3) | copy-start | bytes 8452
  59.7 144.7 %copy-start.63 = (f32[11,64]{1,0:T(8,128)}, f32[11,64]{1,0:T(8,128)S(1)}, u32[]{:S(2)}) copy-start(f32[11,64]{1,0:T(8,128)S(1)} %fusion.64) | copy-start | bytes 8452
  59.7 144.6 %copy-start.51 = (f32[11,64]{1,0:T(8,128)}, f32[11,64]{1,0:T(8,128)S(1)}, u32[]{:S(2)}) copy-start(f32[11,64]{1,0:T(8,128)S(1)} %fusion.119) | copy-start | bytes 8452
  201.4 18.0 %copy-start.39 = (bf16[1,512,512]{2,1,0:T(8,128)(2,1)}, bf16[1,512,512]{2,1,0:T(8,128)(2,1)S(1)}, u32[]{:S(2)}) copy-start(bf16[1,512,512]{2,1,0:T(8,128)(2,1)S(1)} %all-gather.2) | copy-start | bytes 1572868
  221.9 6.3 copy-start.65
  234.1 16.0 %copy-start.53 = (f32[11,64]{1,0:T(8,128)}, f32[11,64]{1,0:T(8,128)S(1)}, u32[]{:S(2)}) copy-start(f32[11,64]{1,0:T(8,128)S(1)} %broadcast_multiply_fusion.1) | copy-start | bytes 8452
  235.6 14.5 %copy-start.67 = (f32[11,64]{1,0:T(8,128)}, f32[11,64]{1,0:T(8,128)S(1)}, u32[]{:S(2)}) copy-start(f32[11,64]{1,0:T(8,128)S(1)} %multiply_reduce_fusion.3) | copy-start | bytes 8452
  235.7 14.5 %copy-start.55 = (f32[11,64]{1,0:T(8,128)}, f32[11,64]{1,0:T(8,128)S(1)}, u32[]{:S(2)}) copy-start(f32[11,64]{1,0:T(8,128)S(1)} %fusion.121) | copy-start | bytes 8452
  284.7 4.4 copy-start.48
  287.1 17.1 %copy-start.57 = (f32[512]{0:T(512)S(1)}, f32[512]{0:T(512)}, u32[]{:S(2)}) copy-start(f32[512]{0:T(512)} %convert_element_type.271) | copy-start | bytes 6148
  289.1 73.6 %copy-start.76 = (f32[11]{0:T(128)S(1)}, f32[11]{0:T(128)}, u32[]{:S(2)}) copy-start(f32[11]{0:T(128)} %fusion.125) | copy-start | bytes 136
  362.8 7.8 copy-start.4
  362.8 7.8 copy-start.38
  386.9 4.4 copy-start.60
  399.9 5.0 copy-start.10
  399.9 5.0 copy-start.12
  420.4 6.5 copy-start.54
  420.4 6.5 copy-start.73
  426.9 4.1 copy-start.7
  426.9 6.4 slice-start
  434.3 7.7 copy-start.20
  434.3 5.0 copy-start.1
  434.3 5.0 copy-start.37
  458.2 264.3 %reduce-scatter.19.cloned.1.call-start = ((), (), s32[]{:S(2)}) async-start(), calls=%async_computation.16 | async-start | bytes 270336
  466.2 6.6 copy-start.15
  466.2 6.6 copy-start.50
  466.2 6.6 copy-start.75
  472.8 4.6 copy-start.52
  479.2 379.0 %reduce-scatter.13.cloned.1.call-start = ((), (), s32[]{:S(2)}) async-start(), calls=%async_computation.7 | async-start | bytes 2162688 | tf_op jit(solution)/shard_map/reduce_scatter | solution.py:228
  480.8 494.8 %reduce-scatter.11.cloned.1.call-start = ((), (), s32[]{:S(2)}) async-start(), calls=%async_computation.6 | async-start | bytes 6488064 | tf_op jit(solution)/shard_map/reduce_scatter | solution.py:227
  489.0 5.3 copy-start.2
  489.0 672.3 %reduce-scatter.15.cloned.1.call-start = ((), (), s32[]{:S(2)}) async-start(), calls=%async_computation.8 | async-start | bytes 8650752 | tf_op jit(solution)/shard_map/reduce_scatter | solution.py:229
  500.3 4.9 copy-start.21
  500.3 848.2 %reduce-scatter.17.cloned.1.call-start = ((), (), s32[]{:S(2)}) async-start(), calls=%async_computation.9 | async-start | bytes 8650752 | tf_op jit(solution)/shard_map/reduce_scatter | solution.py:230
  (49 other events, 100.5 us)
Sparse Core Ops, SparseCore 0:
  11.5 57.7 all-gather.18
  72.8 56.3 all-gather.20
  132.6 55.5 all-gather.22
  191.5 54.0 all-gather.24
  248.9 55.2 all-gather.26
  307.5 55.2 all-gather.28
  458.3 132.2 reduce-scatter.20
  592.9 129.4 reduce-scatter.18
  725.3 132.8 reduce-scatter.12
  865.2 110.3 reduce-scatter.10
  978.5 182.7 reduce-scatter.14
  1164.0 184.4 reduce-scatter.16
where the time goes:
time: 1360 us
  waiting for transfers between devices  901 us (66%)
  blocking collectives  184 us (14%)
  matrix products  118 us (9%)
  local copies, waits for them, and re-layouts  98.6 us (7%)
  other arithmetic  37.3 us (3%)
  between operations  16.2 us (1%)
    unnamed x14, waiting for transfers between devices  199 us
    reduce_scatter x1, waiting for transfers between devices, shards(): lax.psum_scatter(stacked[3], ('wide', 'narrow'), scatter_dimension=1, til...  187 us
    reduce_scatter x1, waiting for transfers between devices, shards(): lax.psum_scatter(stacked[2], ('wide', 'narrow'), scatter_dimension=1, til...  186 us
    reduce_scatter x1, waiting for transfers between devices, shards(): lax.psum_scatter(stacked[1], ('wide', 'narrow'), scatter_dimension=1, til...  134 us
    reduce_scatter x1, waiting for transfers between devices, shards(): lax.psum_scatter(stacked[0], ('wide', 'narrow'), scatter_dimension=1, til...  117 us
    all_gather x1, blocking collectives, shards(): lax.all_gather(temporal_parts[1], ('wide', 'narrow'), axis=0, tiled=True)  74.6 us
    all_gather x1, blocking collectives, shards(): lax.all_gather(spatial_parts[1], ('wide', 'narrow'), axis=0, tiled=True)  67 us
    all_gather x1, waiting for transfers between devices, shards(): lax.all_gather(temporal_parts[3], ('wide', 'narrow'), axis=0, tiled=True)  52.4 us
  transfers between devices with their start and end apart: 12, of which 9 were waited for; matrix products, arithmetic and copies ran while one was open for 11% of the time, Pallas kernels for 0%

commit v1 on v0

--- a/solution.py
+++ b/solution.py
@@ -1,19 +1,1025 @@
+import functools
+
 import jax
 import jax.numpy as jnp
 from jax import lax
+from jax.experimental import pallas as pl
+from jax.experimental.pallas import tpu as pltpu
 from jax.sharding import PartitionSpec as P
 
 HEADS = 8
-
-
-epsilon = 1e-05
+EPS = 1e-05
+BF = jnp.bfloat16
+F32 = jnp.float32
+MESH = pl.DeviceIdType.MESH
+VMEM_LIMIT = 62 * 2**20
+TILE = 256
+
+
+def dot(a, b, ca, cb):
+    return lax.dot_general(a, b, (((ca,), (cb,)), ((), ())), preferred_element_type=F32)
+
+
+def ds(start, size):
+    if isinstance(start, int):
+        return pl.ds(start, size)
+    return pl.ds(pl.multiple_of(start, size), size)
+
+
+def loop(count, body, first=0):
+    def step(i, carry):
+        body(i)
+        return carry
+
+    lax.fori_loop(first, count, step, 0)
+
+
+class Place:
+    def __init__(self, depth):
+        self.depth = depth
+        self.w = lax.axis_index("wide")
+        self.n = lax.axis_index("narrow")
+        self.z = self.w // 2
+        self.c = self.w % 2
+        first = 1 + self.c
+        self.na = self.flip(self.n, first)
+        self.nb = self.flip(self.n, 3 - first)
+        self.nab = 3 - self.n
+
+    @staticmethod
+    def flip(n, step):
+        bit = (n // step) % 2
+        return n + step - 2 * step * bit
+
+    def sib(self):
+        return (self.z * 2 + 1 - self.c, self.n)
+
+    def a(self):
+        return (self.w, self.na)
+
+    def b(self):
+        return (self.w, self.nb)
+
+    def along(self, d):
+        return (lax.rem(self.z + d, self.depth) * 2 + self.c, self.n)
+
+    def zat(self, d):
+        return lax.rem(self.z + d, self.depth)
+
+    def greet(self):
+        bar = pltpu.get_barrier_semaphore()
+        targets = [self.sib(), self.a(), self.b()] + [self.along(d) for d in range(1, self.depth)]
+        for t in targets:
+            pl.semaphore_signal(bar, inc=1, device_id=t, device_id_type=MESH)
+        pl.semaphore_wait(bar, len(targets))
+
+
+def remote(src, dst, send, recv, target):
+    return pltpu.make_async_remote_copy(src, dst, send, recv, device_id=target, device_id_type=MESH)
+
+
+class Gather:
+    def __init__(self, place, full, send, recv):
+        self.p, self.full, self.send, self.recv = place, full, send, recv
+        self.started = []
+
+    def go(self, slot, src_index, dst_index, target):
+        copy = remote(
+            self.full.at[src_index], self.full.at[dst_index], self.send.at[slot], self.recv.at[slot], target
+        )
+        copy.start()
+        self.started.append(copy)
+
+    def take(self, slot, index):
+        view = self.full.at[index]
+        remote(view, view, self.send.at[slot], self.recv.at[slot], self.p.sib()).wait_recv()
+
+    def step0(self):
+        p = self.p
+        own = (p.z, p.c, p.n)
+        for d in range(1, p.depth):
+            self.go(d - 1, own, own, p.along(d))
+
+    def column(self, n, core=None):
+        core = self.p.c if core is None else core
+        return (slice(None), core, n)
+
+    def sibling(self, slot, n):
+        col = self.column(n)
+        self.go(self.p.depth + 2 + slot, col, col, self.p.sib())
+
+    def step1(self):
+        p, base = self.p, self.p.depth - 1
+        for d in range(1, p.depth):
+            self.take(d - 1, (p.zat(p.depth - d), p.c, p.n))
+        col = self.column(p.n)
+        self.go(base, col, col, p.a())
+        self.go(base + 1, col, col, p.b())
+        self.sibling(0, p.n)
+
+    def step2(self):
+        p, base = self.p, self.p.depth - 1
+        self.take(base, self.column(p.na))
+        col = self.column(p.na)
+        self.go(base + 2, col, col, p.b())
+        self.sibling(1, p.na)
+
+    def step3(self):
+        p, base = self.p, self.p.depth - 1
+        self.take(base + 1, self.column(p.nb))
+        self.sibling(2, p.nb)
+        self.take(base + 2, self.column(p.nab))
+        self.sibling(3, p.nab)
+
+    def step4(self):
+        p = self.p
+        for slot, n in enumerate((p.n, p.nb, p.na, p.nab)):
+            self.take(p.depth + 2 + slot, self.column(n, 1 - p.c))
+
+    def finish(self):
+        for copy in self.started:
+            copy.wait_send()
+
+    steps = 5
+
+    def step(self, i):
+        (self.step0, self.step1, self.step2, self.step3, self.step4)[i]()
+
+
+class Scatter:
+    def __init__(self, place, full, from_sib, from_b, from_a, from_z, out, send, recv):
+        self.p, self.full, self.out, self.send, self.recv = place, full, out, send, recv
+        self.from_sib, self.from_b, self.from_a, self.from_z = from_sib, from_b, from_a, from_z
+        self.started = []
+
+    def go(self, slot, src, dst, target):
+        copy = remote(src, dst, self.send.at[slot], self.recv.at[slot], target)
+        copy.start()
+        self.started.append(copy)
+
+    def take(self, slot, view):
+        remote(view, view, self.send.at[slot], self.recv.at[slot], self.p.sib()).wait_recv()
+
+    def add(self, n, part):
+        c = self.p.c
+
+        def body(z):
+            self.full[z, c, n] = self.full[z, c, n] + part(z)
+
+        loop(self.p.depth, body)
+
+    def step0(self):
+        self.go(0, self.full.at[:, 1 - self.p.c], self.from_sib, self.p.sib())
+
+    def step1(self):
+        p = self.p
+        self.take(0, self.from_sib)
+        for slot, n in ((1, p.nab), (2, p.nb)):
+            self.add(n, lambda z, n=n: self.from_sib[z, n])
+            self.go(slot, self.full.at[:, p.c, n], self.from_b.at[slot - 1], p.b())
+        for n in (p.na, p.n):
+            self.add(n, lambda z, n=n: self.from_sib[z, n])
+
+    def step2(self):
+        p = self.p
+        self.take(1, self.from_b.at[0])
+        self.add(p.na, lambda z: self.from_b[0, z])
+        self.go(3, self.full.at[:, p.c, p.na], self.from_a, p.a())
+        self.take(2, self.from_b.at[1])
+        self.add(p.n, lambda z: self.from_b[1, z])
+
+    def step3(self):
+        p = self.p
+        self.take(3, self.from_a)
+        self.add(p.n, lambda z: self.from_a[z])
+        for d in range(1, p.depth):
+            self.go(3 + d, self.full.at[p.zat(d), p.c, p.n], self.from_z.at[d - 1], p.along(d))
+
+    def step4(self):
+        p = self.p
+        total = self.full[p.z, p.c, p.n].astype(F32)
+        for d in range(1, p.depth):
+            self.take(3 + d, self.from_z.at[d - 1])
+            total = total + self.from_z[d - 1].astype(F32)
+        self.out[...] = total
+
+    def finish(self):
+        for copy in self.started:
+            copy.wait_send()
+
+    def step(self, i):
+        (self.step0, self.step1, self.step2, self.step3, self.step4)[i]()
+
+
+def stats(x):
+    centre = jnp.mean(x, axis=-1, keepdims=True)
+    centred = x - centre
+    spread = jnp.mean(centred * centred, axis=-1, keepdims=True)
+    r = lax.rsqrt(spread + EPS)
+    return centred * r, r
+
+
+def norm_into(src, gain, dst, rows):
+    total = src.shape[0]
+
+    def body(i):
+        at = ds(i * rows, rows)
+        xn, _ = stats(src[at, :].astype(F32))
+        dst[at, :] = (xn * gain).astype(BF)
+
+    loop(total // rows, body)
+
+
+def halves(shape):
+    return lax.broadcasted_iota(jnp.int32, shape, 1) < shape[1] // 2
+
+
+def split_heads(x):
+    low = halves(x.shape)
+    zero = jnp.zeros_like(x)
+    return jnp.concatenate([jnp.where(low, x, zero), jnp.where(low, zero, x)], 0)
+
+
+def spatial_forward(qkv, probs, att, patches, width, first, last):
+    head = width // HEADS
+    scale = head ** -0.5
+
+    def body(s):
+        at = ds(s * patches, patches)
+        for pair in range(HEADS // 2):
+            lane = pair * 2 * head
+            q = qkv[at, lane : lane + 2 * head]
+            k2 = split_heads(qkv[at, width + lane : width + lane + 2 * head])
+            v2 = split_heads(qkv[at, 2 * width + lane : 2 * width + lane + 2 * head])
+            scores = dot(q, k2, 1, 1) * scale
+            low = halves(scores.shape)
+            top0 = jnp.max(jnp.where(low, scores, -jnp.inf), axis=-1, keepdims=True)
+            top1 = jnp.max(jnp.where(low, -jnp.inf, scores), axis=-1, keepdims=True)
+            e = jnp.exp(scores - jnp.where(low, top0, top1))
+            sum0 = jnp.sum(jnp.where(low, e, 0.0), axis=-1, keepdims=True)
+            sum1 = jnp.sum(jnp.where(low, 0.0, e), axis=-1, keepdims=True)
+            p = (e / jnp.where(low, sum0, sum1)).astype(BF)
+            probs[s, pair] = p
+            att[at, lane : lane + 2 * head] = dot(p, v2, 1, 0).astype(BF)
+
+    loop(last, body, first)
+
+
+def pad_heads(x, lanes):
+    low = halves(x.shape)
+    zero = jnp.zeros_like(x)
+    fill = jnp.zeros((lanes - x.shape[0], x.shape[1]), x.dtype)
+    return jnp.concatenate([jnp.where(low, x, zero), fill, jnp.where(low, zero, x), fill], 0).astype(BF)
+
+
+LANES = 128
+SUB = 8
+
+
+def temporal_forward(qkv, probs, att, bias, slots, width, first, last):
+    head = width // HEADS
+    scale = head ** -0.5
+    group = slots * SUB
+
+    def body(i):
+        at = ds(i * 2 * group, 2 * group)
+        for pair in range(HEADS // 2):
+            lane = pair * 2 * head
+            q = qkv[at, lane : lane + 2 * head].astype(F32)
+            k = qkv[at, width + lane : width + lane + 2 * head].astype(F32)
+            v = qkv[at, 2 * width + lane : 2 * width + lane + 2 * head].astype(F32)
+            out = []
+            for half in range(2):
+                rows = slice(half * group, (half + 1) * group)
+                scores = dot(q[rows].astype(BF), pad_heads(k[rows], LANES), 1, 1) * scale
+                ps = []
+                for h in range(2):
+                    one = scores[:, h * LANES : (h + 1) * LANES] + bias[...]
+                    e = jnp.exp(one - jnp.max(one, axis=-1, keepdims=True))
+                    ps.append(e / jnp.sum(e, axis=-1, keepdims=True))
+                p = jnp.concatenate(ps, 1).astype(BF)
+                probs[i * 2 + half, pair] = p
+                out.append(dot(p, pad_heads(v[rows], LANES), 1, 0))
+            att[at, lane : lane + 2 * head] = jnp.concatenate(out, 0).astype(BF)
+
+    loop(last, body, first)
+
+
+def make_bias(bias, count, slots):
+    group = slots * SUB
+    q = lax.broadcasted_iota(jnp.int32, (group, LANES), 0)
+    k = lax.broadcasted_iota(jnp.int32, (group, LANES), 1)
+    sq, sk = q // SUB, k // SUB
+    ok = (q - sq * SUB == k - sk * SUB) & (sk <= sq) & (sk < count)
+    bias[...] = jnp.where(ok, 0.0, -1e9)
+
+
+def gelu_pair(z):
+    k0 = 0.7978845608028654
+    z2 = z * z
+    t = jnp.tanh(z * (k0 + (k0 * 0.044715) * z2))
+    half = 0.5 + 0.5 * t
+    slope = half + (0.5 * z) * (1.0 - t * t) * (k0 + (3.0 * k0 * 0.044715) * z2)
+    return z * half, slope
+
+
+def wide_rows(ref, width, columns=None):
+    x = ref[...] if columns is None else ref[:, :, :, :, columns]
+    return x.reshape(width, x.shape[-1])
+
+
+def unsplit_heads(x, second, rows):
+    low = halves((rows, x.shape[1]))
+    return jnp.where(low, x[:rows], x[second : second + rows])
+
+
+def spatial_backward(qkv, probs, grad, patches, width, first, last):
+    head = width // HEADS
+    scale = head ** -0.5
+
+    def body(s):
+        at = ds(s * patches, patches)
+        for pair in range(HEADS // 2):
+            lane = pair * 2 * head
+            cq, ck, cv = (slice(t * width + lane, t * width + lane + 2 * head) for t in range(3))
+            q = qkv[at, cq]
+            k2 = split_heads(qkv[at, ck])
+            v2 = split_heads(qkv[at, cv])
+            g = grad[at, lane : lane + 2 * head]
+            p = probs[s, pair]
+            soft = p.astype(F32)
+            gp = dot(g, v2, 1, 1)
+            low = halves(gp.shape)
+            both = gp * soft
+            sum0 = jnp.sum(jnp.where(low, both, 0.0), axis=-1, keepdims=True)
+            sum1 = jnp.sum(jnp.where(low, 0.0, both), axis=-1, keepdims=True)
+            gs = (soft * (gp - jnp.where(low, sum0, sum1))).astype(BF)
+            qkv[at, cq] = (dot(gs, k2, 1, 0) * scale).astype(BF)
+            qkv[at, ck] = (unsplit_heads(dot(gs, q, 0, 0), patches, patches) * scale).astype(BF)
+            qkv[at, cv] = unsplit_heads(dot(p, g, 0, 0), patches, patches).astype(BF)
+
+    loop(last, body, first)
+
+
+def temporal_backward(qkv, probs, grad, slots, width, first, last):
+    head = width // HEADS
+    scale = head ** -0.5
+    group = slots * SUB
+
+    def body(i):
+        at = ds(i * 2 * group, 2 * group)
+        for pair in range(HEADS // 2):
+            lane = pair * 2 * head
+            cols = [slice(t * width + lane, t * width + lane + 2 * head) for t in range(3)]
+            q, k, v = (qkv[at, c].astype(F32) for c in cols)
+            g = grad[at, lane : lane + 2 * head].astype(F32)
+            outs = ([], [], [])
+            for half in range(2):
+                rows = slice(half * group, (half + 1) * group)
+                gl = g[rows].astype(BF)
+                p = probs[i * 2 + half, pair]
+                gp = dot(gl, pad_heads(v[rows], LANES), 1, 1)
+                parts = []
+                for h in range(2):
+                    lanes = slice(h * LANES, (h + 1) * LANES)
+                    soft = p[:, lanes].astype(F32)
+                    one = gp[:, lanes]
+                    delta = jnp.sum(one * soft, axis=-1, keepdims=True)
+                    parts.append(soft * (one - delta))
+                gs = jnp.concatenate(parts, 1).astype(BF)
+                outs[0].append(dot(gs, pad_heads(k[rows], LANES), 1, 0) * scale)
+                outs[1].append(unsplit_heads(dot(gs, q[rows].astype(BF), 0, 0), LANES, group) * scale)
+                outs[2].append(unsplit_heads(dot(p, gl, 0, 0), LANES, group))
+            for c, o in zip(cols, outs):
+                qkv[at, c] = jnp.concatenate(o, 0).astype(BF)
+
+    loop(last, body, first)
+
+
+def norm_back(src, grad, gain, base, dst, low, sums, rows):
+    total, width = grad.shape
+    sums[...] = jnp.zeros_like(sums)
+
+    def body(i):
+        at = ds(i * rows, rows)
+        xn, r = stats(src[at, :].astype(F32))
+        g = grad[at, :]
+        e = g * gain
+        inner = e - jnp.mean(e, axis=-1, keepdims=True) - xn * jnp.mean(e * xn, axis=-1, keepdims=True)
+        res = base[at, :] + r * inner
+        if dst is not None:
+            dst[at, :] = res
+        low[at, :] = res.astype(BF)
+        sums[...] += jnp.sum((g * xn).reshape(rows // SUB, SUB, width), axis=0)
+
+    loop(total // rows, body)
+
+
+def gain_row(gains, which):
+    return gains[which : which + 1, :]
+
+
+class Sizes:
+    def __init__(self, mesh, video, in_weight):
+        self.depth = mesh.shape["wide"] // 2
+        self.narrow = mesh.shape["narrow"]
+        self.slots, self.patches, self.width = video.shape[1:]
+        self.hidden = in_weight.shape[2]
+        self.tokens = self.slots * self.patches
+        self.group = self.slots * SUB
+        devices = 2 * self.depth * self.narrow
+        w = self.width // devices
+        self.shards = {
+            "qkv": (w, 3 * self.width),
+            "out": (w, self.width),
+            "in": (w, self.hidden),
+            "down": (self.hidden // devices, self.width),
+        }
+        self.mesh_dims = (self.depth, 2, self.narrow)
+
+    def full(self, name):
+        return self.mesh_dims + (TILE_GAIN if name == "gain" else self.shards[name])
+
+    def acts(self, b):
+        t, w, f = self.tokens, self.width, self.hidden
+        pairs = HEADS // 2
+        if b == 0:
+            probs = (self.slots, pairs, self.patches, 2 * self.patches)
+        else:
+            probs = (self.patches // SUB, pairs, self.group, 2 * LANES)
+        return {
+            "normed": ((t, w), BF),
+            "qkv": ((t, 3 * w), BF),
+            "probs": (probs, BF),
+            "att": ((t, w), BF),
+            "middle": ((t, w), F32),
+            "mlp": ((t, w), BF),
+            "active": ((t, f), BF),
+            "slope": ((t, f), BF),
+        }
+
+
+TILE_GAIN = (16, LANES)
+NAMES = ("qkv", "out", "in", "down")
+ACTS = ("normed", "qkv", "probs", "att", "middle", "mlp", "active", "slope")
+GATHER_ORDER = [("gain", 0)] + [(name, b) for b in range(2) for name in NAMES]
+SCATTER_ORDER = [(name, b) for b in (1, 0) for name in ("down", "in", "out", "qkv")] + [("gain", 0)]
+ROWS = 64
+
+
+def keys_of_weights():
+    return [(name, b) for b in range(2) for name in NAMES]
+
+
+def keys_of_acts():
+    return [(name, b) for b in range(2) for name in ACTS]
+
+
+def forward_kernel(sz, plan, *refs):
+    refs = list(refs)
+
+    def grab(n):
+        taken, refs[:n] = refs[:n], []
+        return taken
+
+    video, frames, gain_tile = grab(3)
+    shard = dict(zip(NAMES, grab(4)))
+    (out,) = grab(1)
+    (gains,) = grab(1)
+    h1_hbm, = grab(1)
+    acts_hbm = dict(zip(keys_of_acts(), grab(16)))
+    full_hbm = dict(zip(keys_of_weights(), grab(8)))
+    acts = dict(zip(keys_of_acts(), grab(16)))
+    full = dict(zip(GATHER_ORDER, grab(9)))
+    h1, result, bias, send, recv, local = grab(6)
+    assert not refs
+
+    place = Place(sz.depth)
+    place.greet()
+    gathers = {}
+    for k, key in enumerate(GATHER_ORDER):
+        gathers[key] = Gather(place, full[key], send.at[k], recv.at[k])
+    saved = []
+
+    def save(src, dst):
+        copy = pltpu.make_async_copy(src, dst, local.at[len(saved)])
+        copy.start()
+        saved.append(copy)
+
+    def comm(key, step):
+        if step == 0:
+            own = (place.z, place.c, place.n)
+            if key[0] == "gain":
+                full[key][own] = gain_tile[...]
+            else:
+                full[key][own] = shard[key[0]][key[1]].astype(BF)
+        gathers[key].step(step)
+        if step == 4 and key[0] != "gain":
+            save(full[key], full_hbm[key])
+
+    count = (frames[0] + 1) // 2
+    t, w = sz.tokens, sz.width
+
+    def stage_gain():
+        make_bias(bias, count, sz.slots)
+        tile = jnp.sum(full[("gain", 0)][...].astype(F32).reshape(-1, 16, LANES), axis=0)
+        for g in range(4):
+            rows = [tile[g * 4 + r : g * 4 + r + 1, :] for r in range(w // LANES)]
+            gains[g : g + 1, :] = jnp.concatenate(rows, 1)
+
+    def stages(b):
+        a = {name: acts[(name, b)] for name in ACTS}
+        h = video if b == 0 else h1
+
+        def keep(*names):
+            for name in names:
+                save(a[name], acts_hbm[(name, b)])
+
+        def norm1():
+            norm_into(h, gain_row(gains, 2 * b), a["normed"], ROWS)
+            keep("normed")
+
+        def qkv(first, last):
+            def body(j):
+                at = ds(j * TILE, TILE)
+                a["qkv"][:, at] = dot(a["normed"][...], wide_rows(full[("qkv", b)], w, at), 1, 0).astype(BF)
+
+            loop(last, body, first)
+            if last * TILE == 3 * w:
+                keep("qkv")
+
+        def attend(first, last):
+            if b == 0:
+                spatial_forward(a["qkv"], a["probs"], a["att"], sz.patches, w, first, last)
+                end = sz.slots
+            else:
+                temporal_forward(a["qkv"], a["probs"], a["att"], bias, sz.slots, w, first, last)
+                end = sz.patches // (2 * SUB)
+            if last == end:
+                keep("probs", "att")
+
+        def project():
+            def body(j):
+                at = ds(j * TILE, TILE)
+                new = dot(a["att"][...], wide_rows(full[("out", b)], w, at), 1, 0)
+                a["middle"][:, at] = h[:, at].astype(F32) + new
+
+            loop(w // TILE, body)
+            keep("middle")
+
+        def norm2():
+            norm_into(a["middle"], gain_row(gains, 2 * b + 1), a["mlp"], ROWS)
+            keep("mlp")
+
+        def expand(first, last):
+            def body(j):
+                at = ds(j * TILE, TILE)
+                active, slope = gelu_pair(dot(a["mlp"][...], wide_rows(full[("in", b)], w, at), 1, 0))
+                a["active"][:, at] = active.astype(BF)
+                a["slope"][:, at] = slope.astype(BF)
+
+            loop(last, body, first)
+            if last * TILE == sz.hidden:
+                keep("active", "slope")
+
+        def contract():
+            def body(j):
+                at = ds(j * TILE, TILE)
+                new = a["middle"][:, at] + dot(a["active"][...], wide_rows(full[("down", b)], sz.hidden, at), 1, 0)
+                if b == 0:
+                    new = new.reshape(sz.slots, sz.patches // SUB, SUB, TILE)
+                    for s in range(sz.slots):
+                        h1_view[:, s * SUB : (s + 1) * SUB, at] = new[s]
+                else:
+                    result[:, at] = new
+
+            loop(w // TILE, body)
+            if b == 0:
+                save(h1, h1_hbm)
+
+        def write():
+            valid = lax.broadcasted_iota(jnp.int32, (sz.slots, 1, 1), 0) < count
+
+            def body(i):
+                rows = result[ds(i * 2 * sz.group, 2 * sz.group), :]
+                rows = rows.reshape(2, sz.slots, SUB, w)
+                rows = jnp.concatenate([rows[0], rows[1]], axis=1)
+                out[:, ds(i * 2 * SUB, 2 * SUB), :] = jnp.where(valid, rows, 0.0).astype(BF)
+
+            loop(sz.patches // (2 * SUB), body)
+
+        n_q, n_f = 3 * w // TILE, sz.hidden // TILE
+        n_a = sz.slots if b == 0 else sz.patches // (2 * SUB)
+        cuts = [n_a * i // 4 for i in range(5)]
+        todo = [norm1, lambda: qkv(0, n_q // 2), lambda: qkv(n_q // 2, n_q)]
+        todo += [functools.partial(attend, cuts[i], cuts[i + 1]) for i in range(4)]
+        todo += [project, norm2]
+        todo += [functools.partial(expand, n_f * i // 4, n_f * (i + 1) // 4) for i in range(4)]
+        todo += [contract]
+        if b == 1:
+            todo += [write]
+        return todo
+
+    h1_view = h1.reshape(sz.patches // SUB, sz.group, w)
+    work = iter([stage_gain] + stages(0) + stages(1))
+    for op in plan:
+        if op is None:
+            next(work)()
+        else:
+            comm(GATHER_ORDER[op[0]], op[1])
+    assert next(work, None) is None
+    for gather in gathers.values():
+        gather.finish()
+    for copy in saved:
+        copy.wait()
+
+
+FORWARD_NEEDS = {0: 0, 1: 2, 2: 8, 3: 10, 4: 14, 5: 16, 6: 22, 7: 24, 8: 28}
+FORWARD_STAGES = 30
+
+
+def forward_plan():
+    plan = []
+    for k in range(9):
+        for s in range(5):
+            plan.append((k, s))
+    return plan + [None] * FORWARD_STAGES
+
+
+def backward_kernel(sz, plan, *refs):
+    refs = list(refs)
+
+    def grab(n):
+        taken, refs[:n] = refs[:n], []
+        return taken
+
+    video, cotangent, frames, gains = grab(4)
+    (h1_hbm,) = grab(1)
+    acts_hbm = dict(zip(keys_of_acts(), grab(16)))
+    full_hbm = dict(zip(keys_of_weights(), grab(8)))
+    (grad_video,) = grab(1)
+    outs = dict(zip(NAMES, grab(4)))
+    (gain_out,) = grab(1)
+    acts = dict(zip(ACTS, grab(8)))
+    probs1, h1 = grab(2)
+    full = dict(zip(keys_of_weights(), grab(8)))
+    grads = dict(zip([(name, 1) for name in NAMES] + [("gain", 0)], grab(5)))
+    landing = {key: grab(4) for key in SCATTER_ORDER}
+    grad, grad_mid, grad_norm, low, grad_att, sums = grab(6)
+    send, recv, local_w, local_a = grab(4)
+    assert not refs
+    for name in NAMES:
+        grads[(name, 0)] = full[(name, 1)]
+
+    place = Place(sz.depth)
+    t, w = sz.tokens, sz.width
+    count = (frames[0] + 1) // 2
+    fetched = {}
+
+    def fetch(key, src, dst, sem):
+        copy = pltpu.make_async_copy(src, dst, sem)
+        copy.start()
+        fetched[key] = copy
+
+    def ready(*keys):
+        for key in keys:
+            if key in fetched:
+                fetched.pop(key).wait()
+
+    def act(name, b):
+        return probs1 if (name, b) == ("probs", 1) else acts[name]
+
+    def fetch_act(name, b):
+        i = ACTS.index(name)
+        fetch(("act", name, b), acts_hbm[(name, b)], act(name, b), local_a.at[b, i])
+
+    def fetch_full(name, b):
+        i = NAMES.index(name)
+        fetch(("full", name, b), full_hbm[(name, b)], full[(name, b)], local_w.at[b, i])
+
+    fetch_act("active", 1)
+    fetch_full("down", 1)
+    fetch_act("slope", 1)
+    fetch_act("mlp", 1)
+    fetch_full("in", 1)
+    fetch_act("middle", 1)
+    fetch_act("att", 1)
+    fetch_full("out", 1)
+    fetch_act("qkv", 1)
+    fetch_act("probs", 1)
+    fetch_act("probs", 0)
+    fetch_act("normed", 1)
+    fetch_full("qkv", 1)
+    fetch(("h1",), h1_hbm, h1, local_w.at[0, 4])
+    for name in ("down", "in", "out", "qkv"):
+        fetch_full(name, 0)
+
+    def outs_of(key):
+        return gain_out if key[0] == "gain" else outs[key[0]].at[key[1]]
+
+    place.greet()
+    scatters = {}
+    for k, key in enumerate(SCATTER_ORDER):
+        scatters[key] = Scatter(place, grads[key], *landing[key], outs_of(key), send.at[k], recv.at[k])
+
+    def start():
+        valid = lax.broadcasted_iota(jnp.int32, (sz.slots, 1, 1), 0) < count
+
+        def body(i):
+            rows = cotangent[:, ds(i * 2 * SUB, 2 * SUB), :].astype(F32)
+            rows = jnp.where(valid, rows, 0.0)
+            both = [rows[:, half * SUB : (half + 1) * SUB, :].reshape(sz.group, w) for half in range(2)]
+            rows = jnp.concatenate(both, 0)
+            at = ds(i * 2 * sz.group, 2 * sz.group)
+            grad[at, :] = rows
+            low[at, :] = rows.astype(BF)
+
+        loop(sz.patches // (2 * SUB), body)
+
+    def put_gain(which):
+        row = jnp.sum(sums[...], axis=0, keepdims=True)
+        per = w // LANES
+        tile = jnp.concatenate([row[:, r * LANES : (r + 1) * LANES] for r in range(per)], 0)
+        gain_rows[which * per : (which + 1) * per, :] = tile
+
+    gain_rows = gain_out
+
+    def stages(b):
+        a = {name: act(name, b) for name in ACTS}
+        key = lambda *names: [("act", name, b) for name in names]
+        part = sz.narrow * sz.shards["down"][0]
+
+        def again(*names):
+            if b == 1:
+                for name in names:
+                    fetch_act(name, 0)
+
+        def down_grad(first, last):
+            ready(*key("active"))
+
+            def body(j):
+                g = dot(a["active"][:, ds(j * part, part)], low[...], 0, 0).astype(BF)
+                grads[("down", b)][j // 2, j % 2] = g.reshape(sz.narrow, part // sz.narrow, w)
+
+            loop(last, body, first)
+            if last * part == sz.hidden:
+                again("active")
+
+        def hidden_grad(first, last):
+            ready(("full", "down", b), *key("slope", "mlp"))
+
+            def body(j):
+                at = ds(j * part, part)
+                rows = full[("down", b)][j // 2, j % 2].reshape(part, w)
+                g = dot(low[...], rows, 1, 1) * a["slope"][:, at].astype(F32)
+                g = g.astype(BF)
+                a["slope"][:, at] = g
+                grads[("in", b)][:, :, :, :, at] = dot(a["mlp"][...], g, 0, 0).astype(BF).reshape(
+                    sz.mesh_dims + (sz.shards["in"][0], part)
+                )
+
+            loop(last, body, first)
+            if last * part == sz.hidden:
+                again("mlp")
+
+        def back_rows(src, weight, put):
+            zs = sz.depth // 2
+
+            def body(j):
+                rows = weight[ds(j * zs, zs)]
+                rows = rows.reshape(w // 2, rows.shape[-1])
+                put(ds(j * (w // 2), w // 2), dot(src[...], rows, 1, 1))
+
+            loop(2, body)
+
+        def mlp_back():
+            ready(("full", "in", b))
+
+            def put(at, x):
+                grad_norm[:, at] = x
+
+            back_rows(a["slope"], full[("in", b)], put)
+            again("slope")
+
+        def norm2_back():
+            ready(*key("middle"))
+            norm_back(a["middle"], grad_norm, gain_row(gains, 2 * b + 1), grad, grad_mid, low, sums, ROWS)
+            put_gain(2 * b + 1)
+            again("middle")
+
+        def out_grad():
+            ready(*key("att"))
+
+            def body(j):
+                at = ds(j * TILE, TILE)
+                g = dot(a["att"][...], low[:, at], 0, 0).astype(BF)
+                grads[("out", b)][:, :, :, :, at] = g.reshape(sz.mesh_dims + (sz.shards["out"][0], TILE))
+
+            loop(w // TILE, body)
+            again("att")
+
+        def att_back():
+            ready(("full", "out", b))
+
+            def put(at, x):
+                grad_att[:, at] = x.astype(BF)
+
+            back_rows(low, full[("out", b)], put)
+
+        def attend(first, last):
+            ready(*key("qkv", "probs"))
+            if b == 0:
+                spatial_backward(a["qkv"], a["probs"], grad_att, sz.patches, w, first, last)
+            else:
+                temporal_backward(a["qkv"], a["probs"], grad_att, sz.slots, w, first, last)
+
+        def qkv_grad(first, last):
+            ready(*key("normed"))
+
+            def body(j):
+                at = ds(j * TILE, TILE)
+                g = dot(a["normed"][...], a["qkv"][:, at], 0, 0).astype(BF)
+                grads[("qkv", b)][:, :, :, :, at] = g.reshape(sz.mesh_dims + (sz.shards["qkv"][0], TILE))
+
+            loop(last, body, first)
+            if last * TILE == 3 * w:
+                again("normed")
+
+        def qkv_back():
+            ready(("full", "qkv", b))
+
+            def put(at, x):
+                grad_norm[:, at] = x
+
+            back_rows(a["qkv"], full[("qkv", b)], put)
+            again("qkv")
+
+        def norm1_back():
+            if b == 1:
+                ready(("h1",))
+            src = h1 if b == 1 else video
+            if b == 1:
+                norm_back(src, grad_norm, gain_row(gains, 2), grad_mid, grad, low, sums, ROWS)
+            else:
+                norm_back(src, grad_norm, gain_row(gains, 0), grad_mid, None, grad_video, sums, ROWS)
+            put_gain(2 * b)
+
+        def reorder():
+            view = grad.reshape(sz.patches // SUB, sz.group, w)
+
+            def body(s):
+                rows = view[:, ds(s * SUB, SUB), :].reshape(sz.patches, w)
+                at = ds(s * sz.patches, sz.patches)
+                grad_norm[at, :] = rows
+                low[at, :] = rows.astype(BF)
+
+            loop(sz.slots, body)
+            loop(sz.slots, lambda s: move(ds(s * sz.patches, sz.patches)))
+
+        def move(at):
+            grad[at, :] = grad_norm[at, :]
+
+        n_q, n_f = 3 * w // TILE, sz.hidden // part
+        n_a = sz.slots if b == 0 else sz.patches // (2 * SUB)
+        cuts = [n_a * i // 4 for i in range(5)]
+        todo = []
+        if b == 1:
+            todo += [start]
+        todo += [functools.partial(down_grad, n_f * i // 2, n_f * (i + 1) // 2) for i in range(2)]
+        todo += [functools.partial(hidden_grad, n_f * i // 4, n_f * (i + 1) // 4) for i in range(4)]
+        todo += [mlp_back, norm2_back, out_grad, att_back]
+        todo += [functools.partial(attend, cuts[i], cuts[i + 1]) for i in range(4)]
+        todo += [functools.partial(qkv_grad, n_q * i // 2, n_q * (i + 1) // 2) for i in range(2)]
+        todo += [qkv_back, norm1_back]
+        if b == 1:
+            todo += [reorder]
+        return todo
+
+    def spread_gain():
+        tile = gain_out[...]
+        grads[("gain", 0)][...] = jnp.broadcast_to(tile, sz.full("gain"))
+
+    work = iter(stages(1) + stages(0) + [spread_gain])
+    for op in plan:
+        if op is None:
+            next(work)()
+        else:
+            scatters[SCATTER_ORDER[op[0]]].step(op[1])
+    assert next(work, None) is None
+    for scatter in scatters.values():
+        scatter.finish()
+
+
+BACKWARD_STAGES = 39
+
+
+def backward_plan():
+    plan = [None] * BACKWARD_STAGES
+    for k in range(9):
+        for s in range(5):
+            plan.append((k, s))
+    return plan
+
+
+def gain_tile(attn_gain, mlp_gain, index):
+    own = jnp.stack([attn_gain[0], mlp_gain[0], attn_gain[1], mlp_gain[1]])
+    per = LANES // own.shape[1]
+    values = jnp.repeat(jnp.tile(own, (1, per)), 4, axis=0)
+    row = lax.broadcasted_iota(jnp.int32, values.shape, 0) % 4
+    lane = lax.broadcasted_iota(jnp.int32, values.shape, 1) // own.shape[1]
+    return jnp.where(row * per + lane == index, values, 0.0).astype(BF)
+
+
+def by_kernels(mesh, sz):
+    vmem = pl.BlockSpec(memory_space=pltpu.VMEM)
+    smem = pl.BlockSpec(memory_space=pltpu.SMEM)
+    anyw = pl.BlockSpec(memory_space=pl.ANY)
+    shape = jax.ShapeDtypeStruct
+    t, w = sz.tokens, sz.width
+    act_shapes = [shape(*sz.acts(b)[name]) for b in range(2) for name in ACTS]
+    full_shapes = [shape(sz.full(name), BF) for name, _ in keys_of_weights()]
+    h1_shape = shape((t, w), F32)
+    params = dict(has_side_effects=True, vmem_limit_bytes=VMEM_LIMIT)
+
+    def landing(key):
+        full = sz.full(key[0])
+        kind = F32 if key[0] == "gain" else BF
+        z, _, n, r, c = full
+        return [
+            pltpu.VMEM(s, kind) for s in ((z, n, r, c), (2, z, r, c), (z, r, c), (z - 1, r, c))
+        ]
+
+    def run(video, frames, cotangent, qkv_weight, out_weight, in_weight, down_weight, attn_gain, mlp_gain):
+        index = lax.axis_index("wide") * sz.narrow + lax.axis_index("narrow")
+        tile = gain_tile(attn_gain, mlp_gain, index)
+        rows = video.reshape(t, w)
+        slots = 2 * sz.depth + 6
+        out, gains, h1, *rest = pl.pallas_call(
+            functools.partial(forward_kernel, sz, forward_plan()),
+            out_shape=[shape((sz.slots, sz.patches, w), BF), shape((4, w), F32), h1_shape] + act_shapes + full_shapes,
+            in_specs=[vmem, smem] + [vmem] * 5,
+            out_specs=[vmem, vmem] + [anyw] * 25,
+            scratch_shapes=[pltpu.VMEM(s.shape, s.dtype) for s in act_shapes]
+            + [pltpu.VMEM(sz.full(name), BF) for name, _ in GATHER_ORDER]
+            + [
+                pltpu.VMEM((t, w), F32),
+                pltpu.VMEM((t, w), F32),
+                pltpu.VMEM((sz.group, LANES), F32),
+                pltpu.SemaphoreType.DMA((9, sz.depth + 6)),
+                pltpu.SemaphoreType.DMA((9, sz.depth + 6)),
+                pltpu.SemaphoreType.DMA((25,)),
+            ],
+            compiler_params=pltpu.CompilerParams(collective_id=0, **params),
+        )(rows, frames, tile, qkv_weight, out_weight, in_weight, down_weight)
+        acts0 = sz.acts(0)
+        res = pl.pallas_call(
+            functools.partial(backward_kernel, sz, backward_plan()),
+            out_shape=[shape((t, w), BF)]
+            + [shape((2,) + sz.shards[name], F32) for name in NAMES]
+            + [shape(TILE_GAIN, F32)],
+            in_specs=[vmem, vmem, smem, vmem] + [anyw] * 25,
+            out_specs=[vmem] * 6,
+            scratch_shapes=[pltpu.VMEM(*acts0[name]) for name in ACTS]
+            + [pltpu.VMEM(*sz.acts(1)["probs"]), pltpu.VMEM((t, w), F32)]
+            + [pltpu.VMEM(sz.full(name), BF) for name, _ in keys_of_weights()]
+            + [pltpu.VMEM(sz.full(name), BF) for name in NAMES]
+            + [pltpu.VMEM(sz.full("gain"), F32)]
+            + [buffer for key in SCATTER_ORDER for buffer in landing(key)]
+            + [
+                pltpu.VMEM((t, w), F32),
+                pltpu.VMEM((t, w), F32),
+                pltpu.VMEM((t, w), F32),
+                pltpu.VMEM((t, w), BF),
+                pltpu.VMEM((t, w), BF),
+                pltpu.VMEM((SUB, w), F32),
+                pltpu.SemaphoreType.DMA((9, sz.depth + 3)),
+                pltpu.SemaphoreType.DMA((9, sz.depth + 3)),
+                pltpu.SemaphoreType.DMA((2, 5)),
+                pltpu.SemaphoreType.DMA((2, 8)),
+            ],
+            compiler_params=pltpu.CompilerParams(collective_id=1, **params),
+        )(rows, cotangent.reshape(sz.slots, sz.patches, w), frames, gains, h1, *rest)
+        grad_video, *grads, gain_sums = res
+        per = w // LANES
+        own = attn_gain.shape[1]
+        gain_sums = gain_sums.reshape(4, per * (LANES // own), own)
+        mine = lax.dynamic_index_in_dim(gain_sums, index, 1, keepdims=False)
+        return (
+            out.reshape(video.shape),
+            grad_video.reshape(video.shape),
+            *grads,
+            mine[0::2],
+            mine[1::2],
+        )
+
+    return run
 
 
 def norm_rows(inputs, scaling):
     centre = jnp.mean(inputs, axis=-1, keepdims=True)
     centred = inputs - centre
     spread = jnp.mean(centred * centred, axis=-1, keepdims=True)
-    return centred * lax.rsqrt(spread + epsilon) * scaling
+    return centred * lax.rsqrt(spread + EPS) * scaling
 
 
 def project(rows_in, matrix):
@@ -160,109 +1166,46 @@
     )
 
 
-def pair_stack(first, second):
-    return tuple((jnp.stack([first[number], second[number]]) for number in range(6)))
-
-
-def shards(
+def by_einsums(
     video, frames, cotangent, qkv_weight, out_weight, in_weight, down_weight, attn_gain, mlp_gain
 ):
+    axes = ("wide", "narrow")
     slot_counts = (frames + 1) // 2
     positions = jnp.arange(video.shape[1], dtype=jnp.int32)
     allowed = (positions[None, None, :] <= positions[None, :, None]) & (
         positions[None, None, :] < slot_counts[:, None, None]
     )
     valid_slot = (positions[None, :] < slot_counts[:, None]).astype(jnp.float32)[:, :, None, None]
-    spatial_parts = block_shards(
-        qkv_weight, out_weight, in_weight, down_weight, attn_gain, mlp_gain, 0
-    )
-    temporal_parts = block_shards(
-        qkv_weight, out_weight, in_weight, down_weight, attn_gain, mlp_gain, 1
-    )
-    spatial_full = (
-        lax.all_gather(spatial_parts[0], ("wide", "narrow"), axis=0, tiled=True),
-        lax.all_gather(spatial_parts[1], ("wide", "narrow"), axis=0, tiled=True),
-        lax.all_gather(spatial_parts[2], ("wide", "narrow"), axis=0, tiled=True),
-        lax.all_gather(spatial_parts[3], ("wide", "narrow"), axis=0, tiled=True),
-        lax.all_gather(spatial_parts[4], ("wide", "narrow"), axis=0, tiled=True),
-        lax.all_gather(spatial_parts[5], ("wide", "narrow"), axis=0, tiled=True),
-    )
-    temporal_full = (
-        lax.all_gather(temporal_parts[0], ("wide", "narrow"), axis=0, tiled=True),
-        lax.all_gather(temporal_parts[1], ("wide", "narrow"), axis=0, tiled=True),
-        lax.all_gather(temporal_parts[2], ("wide", "narrow"), axis=0, tiled=True),
-        lax.all_gather(temporal_parts[3], ("wide", "narrow"), axis=0, tiled=True),
-        lax.all_gather(temporal_parts[4], ("wide", "narrow"), axis=0, tiled=True),
-        lax.all_gather(temporal_parts[5], ("wide", "narrow"), axis=0, tiled=True),
-    )
-    start_rows = video.astype(jnp.float32)
-    spatial_out, spatial_stored = block_forward(start_rows, spatial_full, 0, allowed)
-    temporal_out, temporal_stored = block_forward(spatial_out, temporal_full, 1, allowed)
+    weights = (qkv_weight, out_weight, in_weight, down_weight, attn_gain, mlp_gain)
+    full = [
+        tuple(lax.all_gather(part, axes, axis=0, tiled=True) for part in block_shards(*weights, b))
+        for b in range(2)
+    ]
+    spatial_out, spatial_stored = block_forward(video.astype(jnp.float32), full[0], 0, allowed)
+    temporal_out, temporal_stored = block_forward(spatial_out, full[1], 1, allowed)
     output = (temporal_out * valid_slot).astype(jnp.bfloat16)
     gradient = cotangent.astype(jnp.float32) * valid_slot
-    temporal_back = (
-        lax.all_gather(temporal_parts[0], ("wide", "narrow"), axis=0, tiled=True),
-        lax.all_gather(temporal_parts[1], ("wide", "narrow"), axis=0, tiled=True),
-        lax.all_gather(temporal_parts[2], ("wide", "narrow"), axis=0, tiled=True),
-        lax.all_gather(temporal_parts[3], ("wide", "narrow"), axis=0, tiled=True),
-        lax.all_gather(temporal_parts[4], ("wide", "narrow"), axis=0, tiled=True),
-        lax.all_gather(temporal_parts[5], ("wide", "narrow"), axis=0, tiled=True),
-    )
-    grad_between, temporal_grads = block_backward(
-        gradient, temporal_stored, temporal_back, 1, allowed
-    )
-    spatial_back = (
-        lax.all_gather(spatial_parts[0], ("wide", "narrow"), axis=0, tiled=True),
-        lax.all_gather(spatial_parts[1], ("wide", "narrow"), axis=0, tiled=True),
-        lax.all_gather(spatial_parts[2], ("wide", "narrow"), axis=0, tiled=True),
-        lax.all_gather(spatial_parts[3], ("wide", "narrow"), axis=0, tiled=True),
-        lax.all_gather(spatial_parts[4], ("wide", "narrow"), axis=0, tiled=True),
-        lax.all_gather(spatial_parts[5], ("wide", "narrow"), axis=0, tiled=True),
-    )
-    grad_start, spatial_grads = block_backward(
-        grad_between, spatial_stored, spatial_back, 0, allowed
-    )
-    stacked = pair_stack(spatial_grads, temporal_grads)
-    summed = (
-        lax.psum_scatter(stacked[0], ("wide", "narrow"), scatter_dimension=1, tiled=True),
-        lax.psum_scatter(stacked[1], ("wide", "narrow"), scatter_dimension=1, tiled=True),
-        lax.psum_scatter(stacked[2], ("wide", "narrow"), scatter_dimension=1, tiled=True),
-        lax.psum_scatter(stacked[3], ("wide", "narrow"), scatter_dimension=1, tiled=True),
-        lax.psum_scatter(stacked[4], ("wide", "narrow"), scatter_dimension=1, tiled=True),
-        lax.psum_scatter(stacked[5], ("wide", "narrow"), scatter_dimension=1, tiled=True),
-    )
-    return (
-        output,
-        grad_start.astype(jnp.bfloat16),
-        summed[0],
-        summed[1],
-        summed[2],
-        summed[3],
-        summed[4],
-        summed[5],
-    )
+    grad_between, temporal_grads = block_backward(gradient, temporal_stored, full[1], 1, allowed)
+    grad_start, spatial_grads = block_backward(grad_between, spatial_stored, full[0], 0, allowed)
+    summed = [
+        lax.psum_scatter(jnp.stack(pair), axes, scatter_dimension=1, tiled=True)
+        for pair in zip(spatial_grads, temporal_grads)
+    ]
+    return (output, grad_start.astype(jnp.bfloat16), *summed)
 
 
 def solution(mesh):
-    in_specs = (
-        P(("wide", "narrow"), None, None, None),
-        P(("wide", "narrow")),
-        P(("wide", "narrow"), None, None, None),
-        P(None, ("wide", "narrow"), None),
-        P(None, ("wide", "narrow"), None),
-        P(None, ("wide", "narrow"), None),
-        P(None, ("wide", "narrow"), None),
-        P(None, ("wide", "narrow")),
-        P(None, ("wide", "narrow")),
-    )
-    out_specs = (
-        P(("wide", "narrow"), None, None, None),
-        P(("wide", "narrow"), None, None, None),
-        P(None, ("wide", "narrow"), None),
-        P(None, ("wide", "narrow"), None),
-        P(None, ("wide", "narrow"), None),
-        P(None, ("wide", "narrow"), None),
-        P(None, ("wide", "narrow")),
-        P(None, ("wide", "narrow")),
-    )
+    both = ("wide", "narrow")
+    clips = P(both, None, None, None)
+    rows = P(None, both, None)
+    in_specs = (clips, P(both), clips, rows, rows, rows, rows, P(None, both), P(None, both))
+    out_specs = (clips, clips, rows, rows, rows, rows, P(None, both), P(None, both))
+
+    def shards(*args):
+        sz = Sizes(mesh, args[0], args[5])
+        whole_tiles = all(rows % 16 == 0 for rows, _ in sz.shards.values())
+        if whole_tiles and sz.narrow == 4 and args[0].shape[0] == 1:
+            return by_kernels(mesh, sz)(*args)
+        return by_einsums(*args)
+
     return jax.shard_map(shards, mesh=mesh, in_specs=in_specs, out_specs=out_specs, check_vma=False)

time: 1360 us -> 452 us (0.33)
  waiting for transfers between devices: 901 us -> 0 us
  Pallas kernels: 0 us -> 441 us
  blocking collectives: 184 us -> 0 us
  matrix products: 118 us -> 0 us
  local copies, waits for them, and re-layouts: 98.6 us -> 8.49 us
  other arithmetic: 37.3 us -> 0.71 us
  between operations: 16.2 us -> 1.39 us
    reduce_scatter x4 -> x0, waiting for transfers between devices: 625 us -> none  [the longest x1 187 us: shards(): lax.psum_scatter(stacked[3], ('wide', 'narrow'), scatter_dimension=1, til...]
    pallas_call x0 -> x2, Pallas kernels: none -> 441 us  [the longest x1 229 us: run(): pl.pallas_call(functools.partial(backward_kernel, sz, backward_plan()), o...]
    unnamed x14 -> x0, waiting for transfers between devices: 199 us -> none
    all_gather x2 -> x0, blocking collectives: 142 us -> none  [the longest x1 74.6 us: shards(): lax.all_gather(temporal_parts[1], ('wide', 'narrow'), axis=0, tiled=True)]
    dot_general x36 -> x0, matrix products: 118 us -> none  [the longest x8 34.4 us: project(): jnp.einsum('cspd,de->cspe', rows_in, matrix, preferred_element_type=jnp.f...]
    all_gather x6 -> x0, waiting for transfers between devices: 77.4 us -> none  [the longest x1 52.4 us: shards(): lax.all_gather(temporal_parts[3], ('wide', 'narrow'), axis=0, tiled=True)]
    unnamed x1 -> x0, blocking collectives: 42.2 us -> none
    convert_element_type x7 -> x0, local copies, waits for them, and re-layouts: 32.7 us -> none  [the longest x2 13.1 us: block_backward(): jnp.stack([grad_queries, grad_keys, grad_values], axis=3)]
  transfers between devices with their start and end apart: 12 -> 0, of which waited for: 9 -> 0; matrix products, arithmetic and copies ran while one was open for 11% -> 0% of each run, Pallas kernels for 0% -> 0%
where the time goes in v1:
time: 452 us
  Pallas kernels  441 us (98%)
  local copies, waits for them, and re-layouts  8.49 us (2%)
    pallas_call x1, Pallas kernels, run(): pl.pallas_call(functools.partial(backward_kernel, sz, backward_plan()), o...  229 us
    pallas_call x1, Pallas kernels, run(): pl.pallas_call(functools.partial(forward_kernel, sz, forward_plan()), out...  212 us

profile of v1, /device:TPU:0, one launch (start us, length us, event | category | flops | bytes accessed | tf_op | source)
XLA Modules:
  0.0 452.0 jit_solution(13180859880368713856)
XLA Ops:
  1.3 0.8 fusion
  2.1 0.1 tile.10
  2.2 0.7 select_convert_fusion.refs_2_
  2.9 212.4 %shard_map.152 = (bf16[11,64,512]{2,1,0:T(8,128)(2,1)}, f32[4,512]{1,0:T(4,128)}, f32[704,512]{1,0:T(8,128)}, bf16[704,512]{1,0:T(8,128)(2,1)}, bf16[704,1536]{1...) custom-call(bf16[704,512]{1,0:T(8,128)(2,1)} %bitcast.6, ...), custom_call_target="tpu_custom_call" | custom-call | tf_op jit(solution)/shard_map/pallas_call | solution.py:957
  215.3 0.0 copy-start
  215.3 229.1 %shard_map.153 = (bf16[704,512]{1,0:T(8,128)(2,1)}, f32[2,16,1536]{2,1,0:T(8,128)}, f32[2,16,512]{2,1,0:T(8,128)}, f32[2,16,2048]{2,1,0:T(8,128)}, f32[2,64,512]{2,1,0:T(8,128)}, /*index=5*/f32[16,128]{1,0:T(8,128)}) custom-call(bf16[704,512]{1,0:T(8,128)(2,1)} %bitcast.7, bf16[11,64,512]{2,1,0:T(8,128)(2,1)} %bitcast.10, s32[1]{0:T(128)S(6)} %copy.24.refs_1_.refs_2_, ...), custom_call_target="tpu_custom_call" | custom-call | tf_op jit(solution)/shard_map/pallas_call | solution.py:975
  444.3 0.0 copy-start.3
  444.4 0.0 copy-start.4
  444.4 0.0 copy-start.2
  444.4 0.0 copy-start.1
  444.4 0.8 reshape.43
  445.3 0.6 slice.23
  445.8 0.6 slice.22
  446.4 0.0 copy-done
  446.4 0.9 copy.25
  447.3 2.0 copy.26
  449.3 0.0 copy-done.3
  449.3 0.7 copy.27
  450.0 0.0 copy-done.4
  450.0 0.6 copy.28
  450.6 0.0 copy-done.2
  450.6 0.7 copy.29
  451.3 0.0 copy-done.1
  451.3 0.7 copy.30
  (8 shorter events, 0.1 us)
Async XLA Ops:
  215.3 231.2 %copy-start = (bf16[11,64,512]{2,1,0:T(8,128)(2,1)S(1)}, bf16[11,64,512]{2,1,0:T(8,128)(2,1)}, u32[]{:S(2)}) copy-start(bf16[11,64,512]{2,1,0:T(8,128)(2,1)} %get-tuple-element.41) | copy-start | bytes 2162692
  444.3 5.0 %copy-start.3 = (f32[2,16,1536]{2,1,0:T(8,128)S(1)}, f32[2,16,1536]{2,1,0:T(8,128)}, u32[]{:S(2)}) copy-start(f32[2,16,1536]{2,1,0:T(8,128)} %get-tuple-element.94) | copy-start | bytes 589828
  444.4 5.6 %copy-start.4 = (f32[2,16,512]{2,1,0:T(8,128)S(1)}, f32[2,16,512]{2,1,0:T(8,128)}, u32[]{:S(2)}) copy-start(f32[2,16,512]{2,1,0:T(8,128)} %get-tuple-element.95) | copy-start | bytes 196612
  444.4 6.2 %copy-start.2 = (f32[2,16,2048]{2,1,0:T(8,128)S(1)}, f32[2,16,2048]{2,1,0:T(8,128)}, u32[]{:S(2)}) copy-start(f32[2,16,2048]{2,1,0:T(8,128)} %get-tuple-element.96) | copy-start | bytes 786436
  444.4 6.9 %copy-start.1 = (f32[2,64,512]{2,1,0:T(8,128)S(1)}, f32[2,64,512]{2,1,0:T(8,128)}, u32[]{:S(2)}) copy-start(f32[2,64,512]{2,1,0:T(8,128)} %get-tuple-element.97) | copy-start | bytes 786436
